TPU v7x, 256 devices: a whole 4x4x8 slice. The times are simulated.
256 devices in a mesh: grp: 4 (over z_hi, core), dev: 64 (over y, z_lo, x).
Axes of the slice: x: 4, y: 4, z: 8 (z_hi: 2, z_lo: 4; z = z_hi * 4 + z_lo), core: 2. Of those that a mesh axis runs over, the one named last changes fastest.
Arguments:
- images: bfloat16 [512, 16, 16, 768], P(('grp', 'dev')), may hold values from -6 to 6
- cotangent: bfloat16 [512, 16, 16, 768], P(('grp', 'dev')), may hold values from -6 to 6
- dw_kernel: float32 [7, 7, 768], replicated, may hold values from -0.875 to 0.875
- w_expand: bfloat16 [3072, 768], P('dev'), may hold values from -0.21875 to 0.21875
- w_contract: bfloat16 [3072, 768], P('dev'), may hold values from -0.109375 to 0.109375
Outputs:
- block_out: bfloat16 [512, 16, 16, 768], P(('grp', 'dev'))
- grad_images: bfloat16 [512, 16, 16, 768], P(('grp', 'dev'))
- grad_kernel: float32 [7, 7, 768], replicated
- grad_expand: float32 [3072, 768], P('dev')
- grad_contract: float32 [3072, 768], P('dev')
All inputs are finite; a program needn't handle non-finite values.
Results may differ from a plain program's by a relative error of at most 0.0055.
Values may be sent and summed in bfloat16 or wider, within the bound.
A program may use at most 128 MiB of HBM per device.

v0:
```python
import jax
import jax.numpy as jnp
from jax import lax
from jax.sharding import PartitionSpec as P

SQRT_HALF = 0.7071067811865476
INV_ROOT_TWO_PI = 0.3989422804014327
EPSILON = 1e-06


def depthwise(values, kernel):
    side_len = values.shape[1]
    reach = kernel.shape[0] // 2
    padded = jnp.pad(values, ((0, 0), (reach, reach), (reach, reach), (0, 0)))
    result = jnp.zeros(values.shape, jnp.float32)
    for row_off in range(kernel.shape[0]):
        for col_off in range(kernel.shape[1]):
            result = (
                result
                + padded[:, row_off : row_off + side_len, col_off : col_off + side_len, :]
                * kernel[row_off, col_off]
            )
    return result


def conv_back(upstream, kernel):
    side_len = upstream.shape[1]
    reach = kernel.shape[0] // 2
    width = kernel.shape[0] - 1
    padded = jnp.pad(upstream, ((0, 0), (reach, reach), (reach, reach), (0, 0)))
    result = jnp.zeros(upstream.shape, jnp.float32)
    for row_off in range(kernel.shape[0]):
        for col_off in range(kernel.shape[1]):
            result = (
                result
                + padded[
                    :,
                    width - row_off : width - row_off + side_len,
                    width - col_off : width - col_off + side_len,
                    :,
                ]
                * kernel[row_off, col_off]
            )
    return result


def kernel_term(upstream, values, kernel):
    side_len = values.shape[1]
    reach = kernel.shape[0] // 2
    padded = jnp.pad(values, ((0, 0), (reach, reach), (reach, reach), (0, 0)))
    pieces = []
    for row_off in range(kernel.shape[0]):
        for col_off in range(kernel.shape[1]):
            pieces.append(
                jnp.sum(
                    upstream
                    * padded[:, row_off : row_off + side_len, col_off : col_off + side_len, :],
                    axis=(0, 1, 2),
                )
            )
    return jnp.stack(pieces).reshape(kernel.shape)


def reduce_rows(term_fn, hidden):
    dev_count = lax.axis_size("dev")
    shard_sum = lax.psum_scatter(
        term_fn(jnp.int32(0), hidden // dev_count * lax.axis_size("dev")),
        "dev",
        scatter_dimension=0,
        tiled=True,
    )
    return lax.psum(shard_sum, "grp")


def per_device(images, cotangent, dw_kernel, w_expand, w_contract):
    expand, contract = (
        lax.all_gather(w_expand, "dev", axis=0, tiled=True),
        lax.all_gather(w_contract, "dev", axis=0, tiled=True),
    )
    hidden = expand.shape[0]
    channels = images.shape[3]
    tok_rows = images.shape[0] * images.shape[1] * images.shape[2]
    token_total = tok_rows * lax.axis_size("grp") * lax.axis_size("dev")
    grad_scale = float(token_total) ** (-0.5)
    as_float = images.astype(jnp.float32)
    conv_out = depthwise(as_float, dw_kernel).reshape(tok_rows, channels)
    average = jnp.mean(conv_out, axis=1, keepdims=True)
    centred = conv_out - average
    variance = jnp.mean(centred * centred, axis=1, keepdims=True)
    inv_std = lax.rsqrt(variance + EPSILON)
    standard = centred * inv_std
    normed = standard.astype(jnp.bfloat16)
    pre_act = lax.dot_general(
        normed, expand, (((1,), (1,)), ((), ())), preferred_element_type=jnp.float32
    )
    normal_cdf = 0.5 * (1.0 + jax.scipy.special.erf(pre_act * SQRT_HALF))
    activated = (pre_act * normal_cdf).astype(jnp.bfloat16)
    mixed = jnp.dot(activated, contract, preferred_element_type=jnp.float32)
    block_out = (
        (as_float.reshape(tok_rows, channels) + mixed).astype(jnp.bfloat16).reshape(images.shape)
    )
    upstream = cotangent.reshape(tok_rows, channels)
    act_grad = lax.dot_general(
        upstream, contract, (((1,), (1,)), ((), ())), preferred_element_type=jnp.float32
    )
    slope = normal_cdf + pre_act * jnp.exp(-0.5 * pre_act * pre_act) * INV_ROOT_TWO_PI
    pre_grad = (act_grad * slope).astype(jnp.bfloat16)

    def contract_term(offset, length):
        return lax.dot_general(
            activated, upstream, (((0,), (0,)), ((), ())), preferred_element_type=jnp.float32
        )

    grad_contract = reduce_rows(contract_term, hidden) * grad_scale
    norm_grad = jnp.dot(pre_grad, expand, preferred_element_type=jnp.float32)
    conv_grad = inv_std * (
        norm_grad
        - jnp.mean(norm_grad, axis=1, keepdims=True)
        - standard * jnp.mean(norm_grad * standard, axis=1, keepdims=True)
    )
    conv_grad = conv_grad.reshape(images.shape)
    grad_images = (cotangent.astype(jnp.float32) + conv_back(conv_grad, dw_kernel)).astype(
        jnp.bfloat16
    )
    kernel_part = kernel_term(conv_grad, as_float, dw_kernel)
    grad_kernel = lax.psum(kernel_part, ("grp", "dev")) * grad_scale

    def expand_term(offset, length):
        return lax.dot_general(
            pre_grad, normed, (((0,), (0,)), ((), ())), preferred_element_type=jnp.float32
        )

    grad_expand = reduce_rows(expand_term, hidden) * grad_scale
    return (block_out, grad_images, grad_kernel, grad_expand, grad_contract)


def solution(mesh):
    return jax.shard_map(
        per_device,
        mesh=mesh,
        in_specs=(
            P(("grp", "dev"), None, None, None),
            P(("grp", "dev"), None, None, None),
            P(),
            P("dev", None),
            P("dev", None),
        ),
        out_specs=(
            P(("grp", "dev"), None, None, None),
            P(("grp", "dev"), None, None, None),
            P(),
            P("dev", None),
            P("dev", None),
        ),
        check_vma=False,
    )
```

profile of v0, /device:TPU:1, one launch (start us, length us, event | category | flops | bytes accessed | tf_op | source)
XLA Modules:
  0.0 1822.4 jit_solution(178566196506834798)
XLA Ops:
  7.2 0.0 copy-start.5
  7.2 0.0 all-gather.3.cloned.1.call-start
  7.2 0.7 all-gather.3.cloned.1.call-update
  7.9 0.0 all-gather.5.cloned.1.call-start
  8.0 0.7 all-gather.5.cloned.1.call-update
  8.7 0.0 reduce-scatter.3.cloned.1.call-start
  8.7 1.3 convert_element_type.25
  10.0 0.0 copy-done.5
  10.0 0.1 slice_reduce_fusion.46
  10.1 0.2 slice_reduce_fusion.48
  10.3 0.2 slice_reduce_fusion.47
  10.5 11.4 fusion.108
  21.9 0.0 copy-start
  21.9 0.1 div.15
  22.0 0.3 multiply_reduce_fusion.50
  22.3 0.1 rsqrt.12
  22.4 1.1 fusion.106
  23.5 303.8 %all-gather.3.cloned.1.call-done = bf16[3072,768]{1,0:T(8,128)(2,1)} async-done(((bf16[48,768]{1,0:T(8,128)(2,1)}), bf16[3072,768]{1,0:T(8,128)(2,1)}) %all-gather.3.cloned.1.call-update) | async-done | bytes 4718608 | tf_op jit(solution)/shard_map/all_gather | solution.py:77
  327.3 7.0 multiply_convert_fusion
  334.3 347.4 %all-gather.5.cloned.1.call-done = bf16[3072,768]{1,0:T(8,128)(2,1)} async-done(((bf16[48,768]{1,0:T(8,128)(2,1)}), bf16[3072,768]{1,0:T(8,128)(2,1)}) %all-gather.5.cloned.1.call-update) | async-done | bytes 4718608 | tf_op jit(solution)/shard_map/all_gather | solution.py:78
  681.8 0.0 copy-start.4
  681.8 6.9 fusion.5
  688.7 0.0 copy-start.6
  688.7 1.6 copy-done.6
  690.3 0.0 copy-done.4
  690.3 5.1 fusion.109
  695.4 0.0 reduce-scatter.3.cloned.1.call-update
  695.4 0.0 reduce-scatter.5.cloned.1.call-start
  695.4 8.4 fusion.110
  703.8 0.0 reduce-scatter.5.cloned.1.call-update
  703.9 0.2 all-reduce.6.cloned.1.call-start
  704.1 0.0 copy-done
  704.1 6.0 fusion.107
  710.2 6.1 multiply_reduce_fusion.1
  716.5 0.0 copy-start.1
  716.5 3.6 multiply_reduce_fusion
  720.1 0.0 copy-done.1
  720.1 2.4 multiply_reduce_fusion.2
  722.5 0.0 copy-start.3
  722.9 0.3 stack.199
  723.2 0.7 reshape.122
  723.9 0.0 all-reduce.6.cloned.1.call-update
  723.9 0.0 all-reduce.8.cloned.1.call-start
  724.0 0.0 copy-done.3
  724.0 0.0 copy-start.2
  724.0 11.4 fusion.100
  735.4 343.2 %reduce-scatter.3.cloned.1.call-done = f32[48,768]{1,0:T(8,128)} async-done(((f32[3072,768]{1,0:T(8,128)}), f32[48,768]{1,0:T(8,128)}) %reduce-scatter.3.cloned.1.call-update) | async-done | bytes 147472 | tf_op jit(solution)/shard_map/reduce_scatter | solution.py:66
  1078.7 388.5 %reduce-scatter.5.cloned.1.call-done = f32[48,768]{1,0:T(8,128)} async-done(((f32[3072,768]{1,0:T(8,128)}), f32[48,768]{1,0:T(8,128)}) %reduce-scatter.5.cloned.1.call-update) | async-done | bytes 147472 | tf_op jit(solution)/shard_map/reduce_scatter | solution.py:66
  1467.2 0.0 all-reduce.8.cloned.1.call-update
  1467.2 0.0 copy-done.2
  1467.2 6.8 fusion.105
  1474.0 284.0 %all-reduce.6.cloned.1.call-done = f32[7,7,768]{2,1,0:T(8,128)} async-done(((f32[7,7,768]{2,1,0:T(8,128)}), f32[7,7,768]{2,1,0:T(8,128)}) %all-reduce.6.cloned.1.call-update) | async-done | bytes 150544 | tf_op jit(solution)/shard_map/psum | solution.py:126
  1758.0 1.6 broadcast_multiply_fusion
  1759.6 54.2 %all-reduce.8.cloned.1.call-done = (f32[48,768]{1,0:T(8,128)}, f32[48,768]{1,0:T(8,128)}) async-done(((f32[48,768]{1,0:T(8,128)}, f32[48,768]{1,0:T(8,128)}), (f32[48,768]{1,0:T(8,128)}, f32[48,768]{1,0:T(8,128)})) %all-reduce.8.cloned.1.call-update) | async-done | bytes 294928 | tf_op jit(solution)/shard_map/psum | solution.py:72
  1813.8 1.7 broadcast_multiply_fusion.1
  (52 shorter events, 0.2 us)
Async XLA Ops:
  7.2 2.9 copy-start.5
  7.2 320.1 %all-gather.3.cloned.1.call-start = ((), (), s32[]{:S(2)}) async-start(), calls=%async_computation.2 | async-start | bytes 4792320 | tf_op jit(solution)/shard_map/all_gather | solution.py:77
  7.9 673.9 %all-gather.5.cloned.1.call-start = ((), (), s32[]{:S(2)}) async-start(), calls=%async_computation.3 | async-start | bytes 4792320 | tf_op jit(solution)/shard_map/all_gather | solution.py:78
  8.7 1070.0 %reduce-scatter.3.cloned.1.call-start = ((), (), s32[]{:S(2)}) async-start(), calls=%async_computation.5 | async-start | bytes 9584640 | tf_op jit(solution)/shard_map/reduce_scatter | solution.py:66
  21.9 682.2 %copy-start = (f32[2,16,16,768]{3,2,1,0:T(8,128)}, f32[2,16,16,768]{3,2,1,0:T(8,128)S(1)}, u32[]{:S(2)}) copy-start(f32[2,16,16,768]{3,2,1,0:T(8,128)S(1)} %get-tuple-element.109) | copy-start | bytes 4718596
  681.8 8.5 copy-start.4
  688.7 1.6 copy-start.6
  695.4 771.8 %reduce-scatter.5.cloned.1.call-start = ((), (), s32[]{:S(2)}) async-start(), calls=%async_computation.6 | async-start | bytes 9584640 | tf_op jit(solution)/shard_map/reduce_scatter | solution.py:66
  703.9 1054.2 %all-reduce.6.cloned.1.call-start = ((), (), s32[]{:S(2)}) async-start(), calls=%async_computation.4 | async-start | bytes 344064 | tf_op jit(solution)/shard_map/psum | solution.py:126
  716.5 3.6 copy-start.1
  722.5 1.5 copy-start.3
  723.9 1089.9 %all-reduce.8.cloned.1.call-start = ((), (), s32[]{:S(2)}) async-start(), calls=%async_computation.7 | async-start | bytes 589824 | tf_op jit(solution)/shard_map/psum | solution.py:72
  724.0 743.2 %copy-start.2 = (bf16[2,16,16,768]{3,2,1,0:T(8,128)(2,1)S(1)}, bf16[2,16,16,768]{3,2,1,0:T(8,128)(2,1)}, u32[]{:S(2)}) copy-start(bf16[2,16,16,768]{3,2,1,0:T(8,128)(2,1)} %param.5) | copy-start | bytes 2359300
Sparse Core Ops, SparseCore 0:
  9.8 317.4 all-gather.2
  329.1 352.6 all-gather.4
  695.5 383.0 reduce-scatter.2
  1081.1 386.0 reduce-scatter.4
  1473.1 284.8 all-reduce.5
  1760.5 53.2 all-reduce.7
where the time goes:
time: 1820 us
  waiting for transfers between devices  1720 us (95%)
  other arithmetic  41 us (2%)
  matrix products  40.2 us (2%)
    reduce_scatter x2, waiting for transfers between devices, reduce_rows(): lax.psum_scatter(term_fn(jnp.int32(0), hidden // dev_count * lax.axis_siz...  732 us
    all_gather x1, waiting for transfers between devices, per_device(): lax.all_gather(w_contract, 'dev', axis=0, tiled=True)  347 us
    all_gather x1, waiting for transfers between devices, per_device(): lax.all_gather(w_expand, 'dev', axis=0, tiled=True)  304 us
    psum x1, waiting for transfers between devices, per_device(): grad_kernel = lax.psum(kernel_part, ('grp', 'dev')) * grad_scale  284 us
    psum x1, waiting for transfers between devices, reduce_rows(): return lax.psum(shard_sum, 'grp')  54.2 us
  transfers between devices with their start and end apart: 6, of which 6 were waited for; matrix products, arithmetic and copies ran while one was open for 4% of the time, Pallas kernels for 0%

commit v1 on v0

v1 whole, which is shorter than its diff:
```python
import functools

import jax
import jax.numpy as jnp
from jax import lax
from jax.experimental import pallas as pl
from jax.experimental.pallas import tpu as pltpu
from jax.sharding import PartitionSpec as P

MESH = pl.DeviceIdType.MESH
F32, BF16 = jnp.float32, jnp.bfloat16
SQRT_HALF = 0.7071067811865476
INV_ROOT_TWO_PI = 0.3989422804014327
EPSILON = 1e-06
NT = (((1,), (1,)), ((), ()))
NN = (((1,), (0,)), ((), ()))
TN = (((0,), (0,)), ((), ()))

C = 768
TOK = 512
ROWS = 16
ORDERS = (("x", "y", "z"), ("y", "z", "x"), ("z", "x", "y"))
SIZE = {"x": 2, "y": 4, "z": 4}


def dot(a, b, dims):
    return lax.dot_general(a, b, dims, preferred_element_type=F32)


def sizes(part):
    n = [SIZE[a] for a in ORDERS[part]]
    return (1, n[0], n[0] * n[1])


class Place:
    def __init__(self):
        grp, dev = lax.axis_index("grp"), lax.axis_index("dev")
        self.hi, self.core = grp // 2, grp % 2
        self.y, self.zlo, self.x = dev // 16, (dev // 4) % 4, dev % 4
        self.z = self.hi * 4 + self.zlo
        self.source = (self.x % 2) == self.core
        self.other = (self.x % 2) != self.core

    def device(self, x, y, z, core):
        return {"grp": (z // 4) * 2 + core, "dev": (y * 4 + z % 4) * 4 + x}

    def peer(self, axis, off, core=None):
        core = self.core if core is None else core
        x, y, z = self.x, self.y, self.z
        if axis == "x":
            x = (x + off + 4) % 4
        elif axis == "y":
            y = (y + off + 4) % 4
        else:
            z = (z + off + 8) % 8
        return self.device(x, y, z, core)

    def slot(self, axis, off=0):
        if axis == "x":
            return ((self.x + off + 4) % 4) // 2
        if axis == "y":
            return (self.y + off + 4) % 4
        return (self.zlo + off + 4) % 4

    def block(self, part, phase):
        order = ORDERS[part]
        n = [SIZE[a] for a in order]
        i = [self.slot(a) for a in order]
        if phase == 0:
            return (i[2] * n[1] + i[1]) * n[0] + i[0], 1
        if phase == 1:
            return (i[2] * n[1] + i[1]) * n[0], n[0]
        return i[2] * n[1] * n[0], n[0] * n[1]


def moves(axis):
    if axis == "z":
        return ((1, None, 0), (-1, None, 1), (2, 0, 2), (-2, 1, 3))
    return ((1, None, 0), (-1, None, 1), (2, None, 2))


def when(cond, fn):
    if cond is None:
        fn()
    else:
        pl.when(cond)(fn)


def kernel(
    img_ref, cot_ref, dwk_ref, we_ref, wc_ref,
    out_ref, gimg_ref, gker_ref, ge_ref, gc_ref,
    buf, grads, nrm2, cot2, mix, ngr, ex_send, ex_recv, conv, inv, pad, kacc,
    kall, kr0, ksum, krx, ky, kz, fin, finf,
    rb0, rb1, rb2, rb3, rb4, rb5, rb6, rb7, rb8,
    t0, t1, t2, t3, t4, t5, t6, t7, t8,
    bsem_s, bsem_r, rsem_s, rsem_r, esem_s, esem_r, ksem_s, ksem_r, fsem_s, fsem_r,
):
    rbufs = ((rb0, rb1, rb2), (rb3, rb4, rb5), (rb6, rb7, rb8))
    tbufs = ((t0, t1, t2), (t3, t4, t5), (t6, t7, t8))
    at = Place()
    partner = at.device(at.x, at.y, at.z, 1 - at.core)

    barrier = pltpu.get_barrier_semaphore()
    friends = [at.peer("x", o) for o in (1, -1, 2)] + [at.peer("y", o) for o in (1, -1, 2)]
    friends += [at.peer("z", o) for o in range(1, 8)] + [partner]
    friends += [at.peer("x", o, 1 - at.core) for o in (1, -1, 2)]
    for friend in friends:
        pl.semaphore_signal(barrier, inc=1, device_id=friend, device_id_type=MESH)
    pl.semaphore_wait(barrier, len(friends))

    def copy(src, dst, send, recv, to):
        return pltpu.make_async_remote_copy(
            src_ref=src, dst_ref=dst, send_sem=send, recv_sem=recv,
            device_id=to, device_id_type=MESH,
        )

    def gather_copies(part, phase):
        axis = ORDERS[part][phase]
        px = ORDERS[part].index("x")
        start, count = at.block(part, phase)
        out = []
        for off, half, j in moves(axis):
            if half is None:
                ref = buf.at[part, :, pl.ds(start, count)]
            else:
                ref = buf.at[part, half, pl.ds(start, count)]
            cp = copy(ref, ref, bsem_s.at[part, phase, j], bsem_r.at[part, phase, j], at.peer(axis, off))
            if phase < px:
                send_if = recv_if = at.source
            elif phase == px:
                send_if = at.source
                recv_if = at.source if j == 2 else at.other
            else:
                send_if = recv_if = None
            out.append((cp, send_if, recv_if))
        return out

    def gather_start(phase, parts=(0, 1, 2)):
        for part in parts:
            for cp, send_if, _ in gather_copies(part, phase):
                when(send_if, cp.start)

    def gather_wait(phase, parts=(0, 1, 2)):
        for part in parts:
            for cp, send_if, recv_if in gather_copies(part, phase):
                when(send_if, cp.wait_send)
                when(recv_if, cp.wait_recv)

    @pl.when(at.source)
    def _():
        for part in range(3):
            start, _n = at.block(part, 0)
            buf[part, 0, start] = we_ref[part * ROWS : (part + 1) * ROWS]
            buf[part, 1, start] = wc_ref[part * ROWS : (part + 1) * ROWS]

    gather_start(0)
    cot_copy = copy(cot_ref, cot2.at[1], esem_s.at[0], esem_r.at[0], partner)
    cot_copy.start()

    pad[...] = jnp.zeros_like(pad)

    def windows(values):
        pad[3:19, 8:24, :] = values.reshape(16, 16, 128)

    def conv_step(i, source, target, flip, finish):
        image, block = i // 6, i % 6
        lanes = pl.ds(pl.multiple_of(block * 128, 128), 128)
        windows(source[pl.ds(pl.multiple_of(image * 256, 256), 256), lanes].astype(F32))
        for half in range(2):
            acc = jnp.zeros((8, 16, 128), F32)
            for q in range(7):
                shifted = pad[half * 8 : half * 8 + 14, 5 + q : 21 + q, :]
                for p in range(7):
                    tap = 48 - (p * 7 + q) if flip else p * 7 + q
                    acc = acc + shifted[p : p + 8] * dwk_ref[tap : tap + 1, lanes].reshape(1, 1, 128)
            rows = pl.ds(pl.multiple_of(image * 256 + half * 128, 128), 128)
            target[rows, lanes] = finish(acc.reshape(128, 128), rows, lanes)

    def forward(i, carry):
        conv_step(i, img_ref, conv, False, lambda v, rows, lanes: v)

        @pl.when(i == 6)
        def _():
            gather_wait(0)
            gather_start(1)

        return carry

    lax.fori_loop(0, 12, forward, 0)

    def norm(i, carry):
        rows = pl.ds(pl.multiple_of(i * 64, 64), 64)
        v = conv[rows, :]
        centred = v - jnp.mean(v, axis=1, keepdims=True)
        istd = lax.rsqrt(jnp.mean(centred * centred, axis=1, keepdims=True) + EPSILON)
        nrm2[0, rows, :] = (centred * istd).astype(BF16)
        inv[rows, :] = jnp.broadcast_to(istd, (64, 128))
        cot2[0, rows, :] = cot_ref[rows, :]
        mix[0, rows, :] = img_ref[rows, :].astype(F32)
        mix[1, rows, :] = jnp.zeros((64, C), F32)
        ngr[0, rows, :] = jnp.zeros((64, C), F32)
        ngr[1, rows, :] = jnp.zeros((64, C), F32)
        return carry

    lax.fori_loop(0, 8, norm, 0)
    nrm_copy = copy(nrm2.at[0], nrm2.at[1], esem_s.at[1], esem_r.at[1], partner)
    nrm_copy.start()
    gather_wait(1)
    gather_start(2)
    cot_copy.wait()
    nrm_copy.wait()
    gather_wait(2)

    def part_step(part, carry):
        normed = nrm2[...].reshape(2 * TOK, C)
        upstream = cot2[...].reshape(2 * TOK, C)
        expand = buf[part, 0].reshape(512, C)
        contract = buf[part, 1].reshape(512, C)
        pre_act = dot(normed, expand, NT)
        act_grad = dot(upstream, contract, NT)
        cdf = 0.5 * (1.0 + lax.erf(pre_act * SQRT_HALF))
        activated = (pre_act * cdf).astype(BF16)
        slope = cdf + pre_act * jnp.exp(-0.5 * pre_act * pre_act) * INV_ROOT_TWO_PI
        pre_grad = (act_grad * slope).astype(BF16)
        mix[...] += dot(activated, contract, NN).reshape(2, TOK, C)
        ngr[...] += dot(pre_grad, expand, NN).reshape(2, TOK, C)
        grads[part, 0] = dot(pre_grad, normed, TN).astype(BF16).reshape(32, ROWS, C)
        grads[part, 1] = dot(activated, upstream, TN).astype(BF16).reshape(32, ROWS, C)
        return carry

    lax.fori_loop(0, 3, part_step, 0)

    def reduce_copies(part, phase):
        axis = ORDERS[part][phase]
        px = ORDERS[part].index("x")
        count = sizes(part)[phase]
        src = grads.at[part] if phase == 2 else tbufs[part][phase + 1]
        out = []
        for off, half, j in moves(axis):
            pieces = pl.ds(at.slot(axis, off) * count, count)
            if half is None:
                a, b = src.at[:, pieces], rbufs[part][phase].at[j]
            else:
                a, b = src.at[half, pieces], rbufs[part][phase].at[2, half]
            cp = copy(a, b, rsem_s.at[part, phase, j], rsem_r.at[part, phase, j], at.peer(axis, off))
            if phase < px:
                send_if = recv_if = at.source
            elif phase == px:
                send_if = at.source if j == 2 else at.other
                recv_if = at.source
            else:
                send_if = recv_if = None
            out.append((cp, send_if, recv_if))
        return out

    def reduce_start(phase):
        for part in range(3):
            for cp, send_if, _ in reduce_copies(part, phase):
                when(send_if, cp.start)

    def reduce_wait(phase):
        for part in range(3):
            for cp, send_if, recv_if in reduce_copies(part, phase):
                when(send_if, cp.wait_send)
                when(recv_if, cp.wait_recv)
            axis = ORDERS[part][phase]
            count = sizes(part)[phase]
            recv, dst = rbufs[part][phase], tbufs[part][phase]
            mine = at.slot(axis) * count

            def add():
                def piece(i, carry):
                    for side in range(2):
                        if phase == 2:
                            own = grads[part, side, mine + i]
                        else:
                            own = tbufs[part][phase + 1][side, mine + i]
                        total = own.astype(F32) + recv[0, side, i].astype(F32)
                        total = total + recv[1, side, i].astype(F32) + recv[2, side, i].astype(F32)
                        dst[side, i] = total.astype(BF16)
                    return carry

                lax.fori_loop(0, count, piece, 0)

            when(at.source if phase <= ORDERS[part].index("x") else None, add)

    reduce_start(2)

    def to_send(i, carry):
        rows = pl.ds(pl.multiple_of(i * 64, 64), 64)
        ex_send[0, rows, :] = ngr[1, rows, :].astype(BF16)
        ex_send[1, rows, :] = mix[1, rows, :].astype(BF16)
        return carry

    lax.fori_loop(0, 8, to_send, 0)
    ex_copy = copy(ex_send, ex_recv, esem_s.at[2], esem_r.at[2], partner)
    ex_copy.start()
    ex_copy.wait()

    def norm_back(i, carry):
        rows = pl.ds(pl.multiple_of(i * 64, 64), 64)
        out_ref[rows, :] = (mix[0, rows, :] + ex_recv[1, rows, :].astype(F32)).astype(BF16)
        grad = ngr[0, rows, :] + ex_recv[0, rows, :].astype(F32)
        standard = nrm2[0, rows, :].astype(F32)
        mean = jnp.mean(grad, axis=1, keepdims=True)
        along = jnp.mean(grad * standard, axis=1, keepdims=True)
        conv[rows, :] = inv[rows, 0:1] * (grad - mean - standard * along)
        return carry

    lax.fori_loop(0, 8, norm_back, 0)

    def kernel_terms(block, carry):
        lanes = pl.ds(pl.multiple_of(block * 128, 128), 128)
        for image in range(2):
            windows(img_ref[image * 256 : image * 256 + 256, lanes].astype(F32))
            for half in range(2):
                first = image * 256 + half * 128
                g = conv[first : first + 128, lanes].reshape(8, 16, 128)
                for q in range(7):
                    shifted = pad[half * 8 : half * 8 + 14, 5 + q : 21 + q, :]
                    for p in range(7):
                        r = jnp.sum((g * shifted[p : p + 8]).reshape(16, 8, 128), axis=0)
                        if image == 0 and half == 0:
                            kacc[p * 7 + q, :, lanes] = r
                        else:
                            kacc[p * 7 + q, :, lanes] += r
        return carry

    lax.fori_loop(0, 6, kernel_terms, 0)
    kall[49:64, :] = jnp.zeros((15, C), F32)
    kall[0:49, :] = jnp.sum(kacc[...], axis=1)

    k0_copy = copy(kall.at[pl.ds((1 - at.core) * 32, 32)], kr0, ksem_s.at[0], ksem_r.at[0], partner)
    k0_copy.start()

    def kx_copies():
        return [
            copy(ksum.at[pl.ds(((at.x + off + 4) % 4) * 8, 8)], krx.at[j], ksem_s.at[1 + j], ksem_r.at[1 + j], at.peer("x", off))
            for j, off in enumerate((1, -1, 2))
        ]

    def ky_copies():
        return [
            copy(ky.at[at.y], ky.at[at.y], ksem_s.at[4 + j], ksem_r.at[4 + j], at.peer("y", off))
            for j, off in enumerate((1, -1, 2))
        ]

    def kz_copies():
        return [
            copy(kz.at[at.z], kz.at[at.z], ksem_s.at[7 + j], ksem_r.at[7 + j], at.peer("z", off))
            for j, off in enumerate(range(1, 8))
        ]

    share = pl.ds(at.core * 32 + at.x * 8, 8)

    def kg_copies():
        targets = [partner] + [at.peer("x", off, core) for off in (1, -1, 2) for core in (at.core, 1 - at.core)]
        return [copy(finf.at[share], finf.at[share], ksem_s.at[14 + j], ksem_r.at[14 + j], to) for j, to in enumerate(targets)]

    def start_all(copies):
        for cp in copies:
            cp.start()

    def wait_all(copies):
        for cp in copies:
            cp.wait()

    def backward(i, carry):
        conv_step(
            i, conv, gimg_ref, True,
            lambda v, rows, lanes: (v + cot_ref[rows, lanes].astype(F32)).astype(BF16),
        )

        @pl.when(i == 1)
        def _():
            k0_copy.wait()
            ksum[...] = kall[pl.ds(pl.multiple_of(at.core * 32, 32), 32), :] + kr0[...]
            start_all(kx_copies())

        @pl.when(i == 6)
        def _():
            wait_all(kx_copies())
            ky[at.y] = ksum[pl.ds(pl.multiple_of(at.x * 8, 8), 8), :] + krx[0] + krx[1] + krx[2]
            start_all(ky_copies())

        return carry

    lax.fori_loop(0, 12, backward, 0)
    wait_all(ky_copies())
    kz[at.z] = ky[0] + ky[1] + ky[2] + ky[3]
    start_all(kz_copies())

    reduce_wait(2)
    reduce_start(1)
    wait_all(kz_copies())
    total = kz[0]
    for i in range(1, 8):
        total = total + kz[i]
    finf[pl.ds(pl.multiple_of(at.core * 32 + at.x * 8, 8), 8), :] = total
    start_all(kg_copies())
    reduce_wait(1)
    reduce_start(0)
    scale = float(TOK * 256) ** (-0.5)
    wait_all(kg_copies())
    gker_ref[...] = finf[0:49, :] * scale
    reduce_wait(0)

    far = at.peer("z", 4)

    def far_copy():
        return copy(fin.at[at.hi], fin.at[at.hi], fsem_s.at[0], fsem_r.at[0], far)

    def near_copies():
        return [
            copy(ge_ref, ge_ref, fsem_s.at[1], fsem_r.at[1], partner),
            copy(gc_ref, gc_ref, fsem_s.at[2], fsem_r.at[2], partner),
        ]

    @pl.when(at.source)
    def _():
        for part in range(3):
            for side in range(2):
                fin[at.hi, side, part] = tbufs[part][0][side, 0]
        far_copy().start()
        far_copy().wait()
        for side, ref in ((0, ge_ref), (1, gc_ref)):
            for part in range(3):
                total = fin[0, side, part].astype(F32) + fin[1, side, part].astype(F32)
                ref[part * ROWS : (part + 1) * ROWS, :] = total * scale
        for cp in near_copies():
            cp.start()
        for cp in near_copies():
            cp.wait_send()

    @pl.when(at.other)
    def _():
        for cp in near_copies():
            cp.wait_recv()


def per_device(images, cotangent, dw_kernel, w_expand, w_contract):
    vmem = lambda: pl.BlockSpec(memory_space=pltpu.VMEM)
    scratch = [
        pltpu.VMEM((3, 2, 32, ROWS, C), BF16),
        pltpu.VMEM((3, 2, 32, ROWS, C), BF16),
        pltpu.VMEM((2, TOK, C), BF16),
        pltpu.VMEM((2, TOK, C), BF16),
        pltpu.VMEM((2, TOK, C), F32),
        pltpu.VMEM((2, TOK, C), F32),
        pltpu.VMEM((2, TOK, C), BF16),
        pltpu.VMEM((2, TOK, C), BF16),
        pltpu.VMEM((TOK, C), F32),
        pltpu.VMEM((TOK, 128), F32),
        pltpu.VMEM((22, 32, 128), F32),
        pltpu.VMEM((49, 8, C), F32),
        pltpu.VMEM((64, C), F32),
        pltpu.VMEM((32, C), F32),
        pltpu.VMEM((32, C), F32),
        pltpu.VMEM((3, 8, C), F32),
        pltpu.VMEM((4, 8, C), F32),
        pltpu.VMEM((8, 8, C), F32),
        pltpu.VMEM((2, 2, 3, ROWS, C), BF16),
        pltpu.VMEM((64, C), F32),
    ]
    for part in range(3):
        for phase in range(3):
            scratch.append(pltpu.VMEM((3, 2, sizes(part)[phase], ROWS, C), BF16))
    for part in range(3):
        for phase in range(3):
            scratch.append(pltpu.VMEM((2, sizes(part)[phase], ROWS, C), BF16))
    scratch += [pltpu.SemaphoreType.DMA((3, 3, 4))] * 4
    scratch += [pltpu.SemaphoreType.DMA((3,))] * 2
    scratch += [pltpu.SemaphoreType.DMA((21,))] * 2
    scratch += [pltpu.SemaphoreType.DMA((3,))] * 2
    out, gimg, gker, ge, gc = pl.pallas_call(
        kernel,
        name="block_step",
        out_shape=(
            jax.ShapeDtypeStruct((TOK, C), BF16),
            jax.ShapeDtypeStruct((TOK, C), BF16),
            jax.ShapeDtypeStruct((49, C), F32),
            jax.ShapeDtypeStruct((48, C), F32),
            jax.ShapeDtypeStruct((48, C), F32),
        ),
        in_specs=[vmem() for _ in range(5)],
        out_specs=tuple(vmem() for _ in range(5)),
        scratch_shapes=scratch,
        compiler_params=pltpu.CompilerParams(
            collective_id=0, has_side_effects=True, vmem_limit_bytes=63 * 2**20
        ),
        cost_estimate=pl.CostEstimate(flops=15 * 10**9, bytes_accessed=10**7, transcendentals=10**6),
    )(
        images.reshape(TOK, C),
        cotangent.reshape(TOK, C),
        dw_kernel.reshape(49, C),
        w_expand,
        w_contract,
    )
    return out.reshape(images.shape), gimg.reshape(images.shape), gker.reshape(7, 7, C), ge, gc


def solution(mesh):
    tokens = P(("grp", "dev"), None, None, None)
    rows = P("dev", None)
    return jax.shard_map(
        per_device,
        mesh=mesh,
        in_specs=(tokens, tokens, P(), rows, rows),
        out_specs=(tokens, tokens, P(), rows, rows),
        check_vma=False,
    )
```

time: 1820 us -> 121 us (0.07)
  waiting for transfers between devices: 1720 us -> 0 us
  Pallas kernels: 0 us -> 112 us
  other arithmetic: 41 us -> 0 us
  matrix products: 40.2 us -> 0 us
    reduce_scatter x2 -> x0, waiting for transfers between devices: 732 us -> none  [reduce_rows(): lax.psum_scatter(term_fn(jnp.int32(0), hidden // dev_count * lax.axis_siz...]
    all_gather x2 -> x0, waiting for transfers between devices: 651 us -> none  [the longest x1 347 us: per_device(): lax.all_gather(w_contract, 'dev', axis=0, tiled=True)]
    psum x2 -> x0, waiting for transfers between devices: 338 us -> none  [the longest x1 284 us: per_device(): grad_kernel = lax.psum(kernel_part, ('grp', 'dev')) * grad_scale]
    pallas_call x0 -> x1, Pallas kernels: none -> 112 us  [per_device(): pl.pallas_call(kernel, name='block_step', out_shape=(jax.ShapeDtypeStruct...]
    dot_general x6 -> x0, matrix products: 40.2 us -> none  [the longest x1 8.39 us: contract_term(): lax.dot_general(activated, upstream, (((0,), (0,)), ((), ())), preferred_...]
    reduce_sum x5 -> x0, other arithmetic: 23.8 us -> none  [the longest x3 12.1 us: kernel_term(): jnp.sum(upstream * padded[:, row_off:row_off + side_len, col_off:col_off...]
  transfers between devices with their start and end apart: 6 -> 0, of which waited for: 6 -> 0; matrix products, arithmetic and copies ran while one was open for 4% -> 0% of each run, Pallas kernels for 0% -> 0%
where the time goes in v1:
time: 121 us
  Pallas kernels  112 us (93%)
  local copies, waits for them, and re-layouts  8.01 us (7%)
    pallas_call x1, Pallas kernels, per_device(): pl.pallas_call(kernel, name='block_step', out_shape=(jax.ShapeDtypeStruct...  112 us
    unnamed x10, local copies, waits for them, and re-layouts  4.8 us

profile of v1, /device:TPU:1, one launch (start us, length us, event | category | flops | bytes accessed | tf_op | source)
XLA Modules:
  0.0 120.7 jit_solution(6190562366114795012)
XLA Ops:
  0.6 1.6 %reshape.30.dwk_ref = f32[49,768]{1,0:T(8,128)} reshape(f32[7,7,768]{2,1,0:T(8,128)} %param.7) | data formatting | bytes 301056 | tf_op jit(solution)/shard_map/reshape | solution.py:495
  2.2 112.0 %block_step.1 = (bf16[512,768]{1,0:T(8,128)(2,1)}, bf16[512,768]{1,0:T(8,128)(2,1)}, f32[49,768]{1,0:T(8,128)}, f32[48,768]{1,0:T(8,128)}, f32[48,768]{1,0:T(8,128)}) custom-call(bf16[512,768]{1,0:T(8,128)(2,1)} %bitcast.6, bf16[512,768]{1,0:T(8,128)(2,1)} %bitcast.7, f32[49,768]{1,0:T(8,128)} %reshape.30.dwk_ref, bf16[48,768]{1,0:T(8,128)(2,1)} %we_ref.1, ...), custom_call_target="tpu_custom_call" | custom-call | flops 15000000512 | bytes 10000000 | tf_op jit(solution)/shard_map/block_step/pallas_call | solution.py:475
  114.3 1.6 %reshape.33 = f32[7,7,768]{2,1,0:T(8,128)} reshape(f32[49,768]{1,0:T(8,128)} %get-tuple-element.12) | data formatting | bytes 301056 | tf_op jit(solution)/shard_map/reshape | solution.py:499
  115.9 0.0 copy-start
  115.9 2.1 %copy.14 = bf16[2,16,16,768]{3,2,1,0:T(8,128)(2,1)} copy(bf16[2,16,16,768]{3,2,1,0:T(8,128)(2,1)} %bitcast.5) | data formatting | bytes 1572864
  118.0 0.0 copy-done
  118.0 0.0 copy-start.2
  118.0 0.9 copy.15
  118.9 0.1 copy-done.2
  119.0 0.0 copy-start.1
  119.0 0.7 copy.16
  119.7 0.3 copy-done.1
  120.0 0.7 copy.17
Async XLA Ops:
  115.9 2.1 %copy-start = (bf16[512,768]{1,0:T(8,128)(2,1)S(1)}, bf16[512,768]{1,0:T(8,128)(2,1)}, u32[]{:S(2)}) copy-start(bf16[512,768]{1,0:T(8,128)(2,1)} %get-tuple-element.11) | copy-start | bytes 2359300
  118.0 1.0 copy-start.2
  119.0 1.0 copy-start.1

commit v2 on v1

v2 whole, which is shorter than its diff:
```python
import functools

import jax
import jax.numpy as jnp
from jax import lax
from jax.experimental import pallas as pl
from jax.experimental.pallas import tpu as pltpu
from jax.sharding import PartitionSpec as P

MESH = pl.DeviceIdType.MESH
F32, BF16 = jnp.float32, jnp.bfloat16
SQRT_HALF = 0.7071067811865476
INV_ROOT_TWO_PI = 0.3989422804014327
EPSILON = 1e-06
NT = (((1,), (1,)), ((), ()))
NN = (((1,), (0,)), ((), ()))
TN = (((0,), (0,)), ((), ()))

C = 768
TOK = 512
ROWS = 16
SPLIT = 4
ORDERS = (("x", "y", "z"), ("y", "z", "x"), ("z", "x", "y"))
SIZE = {"x": 2, "y": 4, "z": 4}


def dot(a, b, dims):
    return lax.dot_general(a, b, dims, preferred_element_type=F32)


def sizes(part):
    n = [SIZE[a] for a in ORDERS[part]]
    return (1, n[0], n[0] * n[1])


class Place:
    def __init__(self):
        grp, dev = lax.axis_index("grp"), lax.axis_index("dev")
        self.hi, self.core = grp // 2, grp % 2
        self.y, self.zlo, self.x = dev // 16, (dev // 4) % 4, dev % 4
        self.z = self.hi * 4 + self.zlo
        self.source = (self.x % 2) == self.core
        self.other = (self.x % 2) != self.core

    def device(self, x, y, z, core):
        return {"grp": (z // 4) * 2 + core, "dev": (y * 4 + z % 4) * 4 + x}

    def peer(self, axis, off, core=None):
        core = self.core if core is None else core
        x, y, z = self.x, self.y, self.z
        if axis == "x":
            x = (x + off + 4) % 4
        elif axis == "y":
            y = (y + off + 4) % 4
        else:
            z = (z + off + 8) % 8
        return self.device(x, y, z, core)

    def slot(self, axis, off=0):
        if axis == "x":
            return ((self.x + off + 4) % 4) // 2
        if axis == "y":
            return (self.y + off + 4) % 4
        return (self.zlo + off + 4) % 4

    def share(self, part, step):
        first = (self.y, self.zlo, 2 * (self.x // 2))[part]
        return (first + step) % SPLIT

    def runs(self, part, phase):
        order = ORDERS[part]
        n = [SIZE[a] for a in order]
        i = [self.slot(a) for a in order]
        share = n[0] * n[1] // SPLIT
        if phase == 1:
            first, count = i[1] * n[0], n[0]
        else:
            first, count = i[1] * n[0] + i[0], 1
        step = min(count, share)
        return [
            (where(part, (first + k) // share, i[2]) + (first + k) % share, step)
            for k in range(0, count, step)
        ]


def where(part, s, i3):
    share = sizes(part)[2] // SPLIT
    return s * (96 // SPLIT) + part * (32 // SPLIT) + i3 * share


def moves(axis):
    if axis == "z":
        return ((1, None, 0), (-1, None, 1), (2, 0, 2), (-2, 1, 3))
    return ((1, None, 0), (-1, None, 1), (2, None, 2))


def when(cond, fn):
    if cond is None:
        fn()
    else:
        pl.when(cond)(fn)


def kernel(
    img_hbm, cot_hbm, dwk_ref, we_ref, wc_ref,
    out_hbm, gimg_hbm, gker_ref, ge_ref, gc_ref,
    img_ref, out_ref, gimg_ref, buf, grads, nrm2, cot2, mix, ngr, ex_send, ex_recv, conv, inv, pad, kacc,
    kall, krx, ky, kz, fin, finf,
    rb0, rb1, rb2, rb3, rb4, rb5, rb6, rb7, rb8,
    t0, t1, t2, t3, t4, t5, t6, t7, t8,
    bsem_s, bsem_r, rsem_s, rsem_r, esem_s, esem_r, ksem_s, ksem_r, fsem_s, fsem_r, lsem,
):
    rbufs = ((rb0, rb1, rb2), (rb3, rb4, rb5), (rb6, rb7, rb8))
    tbufs = ((t0, t1, t2), (t3, t4, t5), (t6, t7, t8))
    at = Place()
    partner = at.device(at.x, at.y, at.z, 1 - at.core)

    barrier = pltpu.get_barrier_semaphore()
    friends = [at.peer("x", o) for o in (1, -1, 2)] + [at.peer("y", o) for o in (1, -1, 2)]
    friends += [at.peer("z", o) for o in range(1, 8)] + [partner]
    friends += [at.peer("x", o, 1 - at.core) for o in (1, -1, 2)]
    for friend in friends:
        pl.semaphore_signal(barrier, inc=1, device_id=friend, device_id_type=MESH)
    img_in = pltpu.make_async_copy(img_hbm, img_ref, lsem.at[0])
    cot_in = pltpu.make_async_copy(cot_hbm, cot2.at[0], lsem.at[1])
    img_in.start()
    cot_in.start()
    pl.semaphore_wait(barrier, len(friends))

    def copy(src, dst, send, recv, to):
        return pltpu.make_async_remote_copy(
            src_ref=src, dst_ref=dst, send_sem=send, recv_sem=recv,
            device_id=to, device_id_type=MESH,
        )

    def gather_copies(part, phase, step=None):
        axis = ORDERS[part][phase]
        px = ORDERS[part].index("x")
        if phase == 2:
            share = at.share(part, step)
            runs = [(step, (where(part, share, at.slot(axis)), sizes(part)[2] // SPLIT))]
        else:
            runs = enumerate(at.runs(part, phase))
        out = []
        for r, (start, count) in runs:
            for off, half, j in moves(axis):
                if half is None:
                    ref = buf.at[:, pl.ds(start, count)]
                else:
                    ref = buf.at[half, pl.ds(start, count)]
                cp = copy(ref, ref, bsem_s.at[part, phase, r, j], bsem_r.at[part, phase, r, j], at.peer(axis, off))
                if phase < px:
                    send_if = recv_if = at.source
                elif phase == px:
                    send_if = at.source
                    recv_if = at.source if j == 2 else at.other
                else:
                    send_if = recv_if = None
                out.append((cp, send_if, recv_if))
        return out

    def gather_start(part, phase, step=None):
        for cp, send_if, _ in gather_copies(part, phase, step):
            when(send_if, cp.start)

    def gather_wait(part, phase, step=None):
        for cp, send_if, recv_if in gather_copies(part, phase, step):
            when(send_if, cp.wait_send)
            when(recv_if, cp.wait_recv)

    def gather_second():
        for part in range(3):
            gather_wait(part, 0)
        for part in range(3):
            gather_start(part, 1)
        gather_start(0, 2, 0)
        gather_start(1, 2, 0)

        @pl.when(at.source)
        def _():
            gather_start(2, 2, 0)
            gather_start(2, 2, 1)

    def gather_third():
        for part in range(3):
            gather_wait(part, 1)

        @pl.when(at.other)
        def _():
            gather_start(2, 2, 0)

        gather_start(0, 2, 1)
        gather_start(1, 2, 1)

        @pl.when(at.other)
        def _():
            gather_start(2, 2, 1)

        for step in range(2, SPLIT):
            for part in range(3):
                gather_start(part, 2, step)

    @pl.when(at.source)
    def _():
        for part in range(3):
            ((start, _n),) = at.runs(part, 0)
            buf[0, start] = we_ref[part * ROWS : (part + 1) * ROWS]
            buf[1, start] = wc_ref[part * ROWS : (part + 1) * ROWS]

    for part in range(3):
        gather_start(part, 0)
    cot_copy = copy(cot_hbm, cot2.at[1], esem_s.at[0], esem_r.at[0], partner)
    cot_copy.start()

    pad[...] = jnp.zeros_like(pad)
    img_in.wait()

    def windows(values):
        pad[3:19, 8:24, :] = values.reshape(16, 16, 128)

    def conv_step(i, source, target, flip, finish):
        image, block = i // 6, i % 6
        lanes = pl.ds(pl.multiple_of(block * 128, 128), 128)
        windows(source[pl.ds(pl.multiple_of(image * 256, 256), 256), lanes].astype(F32))
        for half in range(2):
            acc = jnp.zeros((8, 16, 128), F32)
            for q in range(7):
                shifted = pad[half * 8 : half * 8 + 14, 5 + q : 21 + q, :]
                for p in range(7):
                    tap = 48 - (p * 7 + q) if flip else p * 7 + q
                    acc = acc + shifted[p : p + 8] * dwk_ref[tap // 7, tap % 7 : tap % 7 + 1, lanes].reshape(1, 1, 128)
            rows = pl.ds(pl.multiple_of(image * 256 + half * 128, 128), 128)
            target[rows, lanes] = finish(acc.reshape(128, 128), rows, lanes)

    def forward(i, carry):
        conv_step(i, img_ref, conv, False, lambda v, rows, lanes: v)

        @pl.when(i == 6)
        def _():
            gather_second()

        return carry

    lax.fori_loop(0, 12, forward, 0)

    def norm(i, carry):
        rows = pl.ds(pl.multiple_of(i * 64, 64), 64)
        v = conv[rows, :]
        centred = v - jnp.mean(v, axis=1, keepdims=True)
        istd = lax.rsqrt(jnp.mean(centred * centred, axis=1, keepdims=True) + EPSILON)
        nrm2[0, rows, :] = (centred * istd).astype(BF16)
        inv[rows, :] = jnp.broadcast_to(istd, (64, 128))
        mix[0, rows, :] = img_ref[rows, :].astype(F32)
        mix[1, rows, :] = jnp.zeros((64, C), F32)
        ngr[0, rows, :] = jnp.zeros((64, C), F32)
        ngr[1, rows, :] = jnp.zeros((64, C), F32)
        return carry

    lax.fori_loop(0, 8, norm, 0)
    nrm_copy = copy(nrm2.at[0], nrm2.at[1], esem_s.at[1], esem_r.at[1], partner)
    nrm_copy.start()
    gather_third()
    cot_in.wait()
    cot_copy.wait()
    nrm_copy.wait()

    def sides(part, phase):
        px = ORDERS[part].index("x")
        if phase < px:
            return (at.source,) * 4
        if phase == px:
            return at.other, at.source, at.source, at.source
        return (None,) * 4

    def reduce_last(part, step):
        axis = ORDERS[part][2]
        send_1, recv_1, send_2, recv_2 = sides(part, 2)
        share, count = at.share(part, step), sizes(part)[2] // SPLIT
        out = []
        for off, half, j in moves(axis):
            pieces = pl.ds(where(part, share, at.slot(axis, off)), count)
            lands = pl.ds(share * count, count)
            if half is None:
                a, b = grads.at[:, pieces], rbufs[part][2].at[j, :, lands]
            else:
                a, b = grads.at[half, pieces], rbufs[part][2].at[2, half, lands]
            cp = copy(a, b, rsem_s.at[part, 2, step, j], rsem_r.at[part, 2, step, j], at.peer(axis, off))
            out.append((cp, send_2 if j >= 2 else send_1, recv_2 if j >= 2 else recv_1))
        return out

    def reduce_middle(part, share, q):
        axis = ORDERS[part][1]
        send_1, recv_1, send_2, recv_2 = sides(part, 1)
        count = sizes(part)[2] // SPLIT
        per_block = sizes(part)[1] // count
        out = []
        for off, half, j in moves(axis):
            pieces, lands = pl.ds(share * count, count), pl.ds(q * count, count)
            src, dst = tbufs[part][2], rbufs[part][1]
            if half is None:
                a, b = src.at[:, pieces], dst.at[j, :, lands]
            else:
                a, b = src.at[half, pieces], dst.at[2, half, lands]
            cp = copy(a, b, rsem_s.at[part, 1, q, j], rsem_r.at[part, 1, q, j], at.peer(axis, off))
            goes = at.slot(axis, off) == share // per_block
            out.append((cp, goes, send_2 if j >= 2 else send_1, recv_2 if j >= 2 else recv_1))
        return out

    def reduce_first(part):
        axis = ORDERS[part][0]
        send_1, recv_1, send_2, recv_2 = sides(part, 0)
        out = []
        for off, half, j in moves(axis):
            pieces = pl.ds(at.slot(axis, off), 1)
            src, dst = tbufs[part][1], rbufs[part][0]
            if half is None:
                a, b = src.at[:, pieces], dst.at[j]
            else:
                a, b = src.at[half, pieces], dst.at[2, half]
            cp = copy(a, b, rsem_s.at[part, 0, 0, j], rsem_r.at[part, 0, 0, j], at.peer(axis, off))
            out.append((cp, send_2 if j >= 2 else send_1, recv_2 if j >= 2 else recv_1))
        return out

    def add_up(count, first, own, own_first, recv, dst):
        def piece(i, carry):
            for side in range(2):
                total = own[side, own_first + i].astype(F32) + recv[0, side, first + i].astype(F32)
                total = total + recv[1, side, first + i].astype(F32) + recv[2, side, first + i].astype(F32)
                dst[side, first + i] = total.astype(BF16)
            return carry

        lax.fori_loop(0, count, piece, 0)

    def reduce_start_last(step):
        for part in range(3):
            for cp, send_if, _ in reduce_last(part, step):
                when(send_if, cp.start)

    def reduce_second(step):
        for part in range(3):
            for cp, send_if, recv_if in reduce_last(part, step):
                when(send_if, cp.wait_send)
                when(recv_if, cp.wait_recv)
            share, count = at.share(part, step), sizes(part)[2] // SPLIT
            per_block = sizes(part)[1] // count

            def go(part=part, share=share, count=count, per_block=per_block):
                mine = where(part, share, at.slot(ORDERS[part][2]))
                add_up(count, share * count, grads, mine, rbufs[part][2], tbufs[part][2])
                for cp, goes, send_if, _ in reduce_middle(part, share, share % per_block):
                    when(goes if send_if is None else jnp.logical_and(goes, send_if), cp.start)

            when(at.source if ORDERS[part][2] == "x" else None, go)

    def reduce_third():
        for part in range(3):
            count = sizes(part)[2] // SPLIT
            per_block = sizes(part)[1] // count
            for q in range(per_block):
                for cp, _, send_if, recv_if in reduce_middle(part, q, q):
                    when(send_if, cp.wait_send)
                    when(recv_if, cp.wait_recv)

            def go(part=part):
                n1 = sizes(part)[1]
                add_up(n1, 0, tbufs[part][2], at.slot(ORDERS[part][1]) * n1, rbufs[part][1], tbufs[part][1])

            when(at.source if ORDERS[part].index("x") >= 1 else None, go)
            for cp, send_if, _ in reduce_first(part):
                when(send_if, cp.start)

    def reduce_end():
        for part in range(3):
            for cp, send_if, recv_if in reduce_first(part):
                when(send_if, cp.wait_send)
                when(recv_if, cp.wait_recv)

            def go(part=part):
                add_up(1, 0, tbufs[part][1], at.slot(ORDERS[part][0]), rbufs[part][0], tbufs[part][0])

            when(at.source, go)

    count = 32 // SPLIT
    width = 3 * count * ROWS

    def share_step(step, carry):
        for part in range(3):
            gather_wait(part, 2, step)
        normed = nrm2[...].reshape(2 * TOK, C)
        upstream = cot2[...].reshape(2 * TOK, C)
        here = [pl.ds(where(part, at.share(part, step), 0), count) for part in range(3)]
        expand = jnp.concatenate([buf[0, h] for h in here]).reshape(width, C)
        contract = jnp.concatenate([buf[1, h] for h in here]).reshape(width, C)
        pre_act = dot(normed, expand, NT)
        act_grad = dot(upstream, contract, NT)
        cdf = 0.5 * (1.0 + lax.erf(pre_act * SQRT_HALF))
        activated = (pre_act * cdf).astype(BF16)
        slope = cdf + pre_act * jnp.exp(-0.5 * pre_act * pre_act) * INV_ROOT_TWO_PI
        pre_grad = (act_grad * slope).astype(BF16)
        grad_e = dot(pre_grad, normed, TN).astype(BF16).reshape(3, count, ROWS, C)
        grad_c = dot(activated, upstream, TN).astype(BF16).reshape(3, count, ROWS, C)
        for part in range(3):
            grads[0, here[part]] = grad_e[part]
            grads[1, here[part]] = grad_c[part]
        reduce_start_last(step)
        ngr[...] += dot(pre_grad, expand, NN).reshape(2, TOK, C)
        mix[...] += dot(activated, contract, NN).reshape(2, TOK, C)

        @pl.when(step >= 2)
        def _():
            reduce_second(step - 2)

        return carry

    lax.fori_loop(0, SPLIT, share_step, 0)
    def send_back(i, source):
        def to_send(k, carry):
            rows = pl.ds(pl.multiple_of(k * 64, 64), 64)
            ex_send[i, rows, :] = source[1, rows, :].astype(BF16)
            return carry

        lax.fori_loop(0, 8, to_send, 0)
        cp = copy(ex_send.at[i], ex_recv.at[i], esem_s.at[2 + i], esem_r.at[2 + i], partner)
        cp.start()
        return cp

    ngr_copy = send_back(0, ngr)
    mix_copy = send_back(1, mix)
    ngr_copy.wait()
    def norm_back(i, carry):
        rows = pl.ds(pl.multiple_of(i * 64, 64), 64)
        grad = ngr[0, rows, :] + ex_recv[0, rows, :].astype(F32)
        standard = nrm2[0, rows, :].astype(F32)
        mean = jnp.mean(grad, axis=1, keepdims=True)
        along = jnp.mean(grad * standard, axis=1, keepdims=True)
        conv[rows, :] = inv[rows, 0:1] * (grad - mean - standard * along)
        return carry

    lax.fori_loop(0, 8, norm_back, 0)

    def kernel_terms(block, carry):
        @pl.when(block % 3 == 0)
        def _():
            reduce_second(2 + block // 3)

        lanes = pl.ds(pl.multiple_of(block * 128, 128), 128)
        for image in range(2):
            windows(img_ref[image * 256 : image * 256 + 256, lanes].astype(F32))
            for half in range(2):
                first = image * 256 + half * 128
                g = conv[first : first + 128, lanes].reshape(8, 16, 128)
                for q in range(7):
                    shifted = pad[half * 8 : half * 8 + 14, 5 + q : 21 + q, :]
                    for p in range(7):
                        r = jnp.sum((g * shifted[p : p + 8]).reshape(16, 8, 128), axis=0)
                        if image == 0 and half == 0:
                            kacc[p * 7 + q, :, lanes] = r
                        else:
                            kacc[p * 7 + q, :, lanes] += r
        return carry

    lax.fori_loop(0, 6, kernel_terms, 0)
    kall[49:64, :] = jnp.zeros((15, C), F32)
    kall[0:49, :] = jnp.sum(kacc[...], axis=1)

    plane = [(0, 1 - at.core)] + [(off, core) for off in (1, -1, 2) for core in (at.core, 1 - at.core)]

    def kx_copies():
        out = []
        for j, (off, core) in enumerate(plane):
            rows = pl.ds(core * 32 + ((at.x + off + 4) % 4) * 8, 8)
            out.append(copy(kall.at[rows], krx.at[j], ksem_s.at[j], ksem_r.at[j], at.peer("x", off, core)))
        return out

    def ky_copies():
        return [
            copy(ky.at[at.y], ky.at[at.y], ksem_s.at[7 + j], ksem_r.at[7 + j], at.peer("y", off))
            for j, off in enumerate((1, -1, 2))
        ]

    def kz_copies():
        return [
            copy(kz.at[at.z], kz.at[at.z], ksem_s.at[10 + j], ksem_r.at[10 + j], at.peer("z", off))
            for j, off in enumerate(range(1, 8))
        ]

    share = pl.ds(at.core * 32 + at.x * 8, 8)

    def kg_copies():
        return [
            copy(finf.at[share], finf.at[share], ksem_s.at[17 + j], ksem_r.at[17 + j], at.peer("x", off, core))
            for j, (off, core) in enumerate(plane)
        ]

    def start_all(copies):
        for cp in copies:
            cp.start()

    def wait_all(copies):
        for cp in copies:
            cp.wait()

    start_all(kx_copies())
    mix_copy.wait()

    def block_out(i, carry):
        rows = pl.ds(pl.multiple_of(i * 64, 64), 64)
        out_ref[rows, :] = (mix[0, rows, :] + ex_recv[1, rows, :].astype(F32)).astype(BF16)
        return carry

    lax.fori_loop(0, 8, block_out, 0)
    block_copy = pltpu.make_async_copy(out_ref, out_hbm, lsem.at[2])
    block_copy.start()

    scale = float(TOK * 256) ** (-0.5)

    far = at.peer("z", 4)

    def far_copy():
        return copy(fin.at[at.hi], fin.at[at.hi], fsem_s.at[0], fsem_r.at[0], far)

    def near_copies():
        return [
            copy(ge_ref, ge_ref, fsem_s.at[1], fsem_r.at[1], partner),
            copy(gc_ref, gc_ref, fsem_s.at[2], fsem_r.at[2], partner),
        ]

    def far_start():
        @pl.when(at.source)
        def _():
            for part in range(3):
                for side in range(2):
                    fin[at.hi, side, part] = tbufs[part][0][side, 0]
            far_copy().start()

    def backward(i, carry):
        conv_step(
            i, conv, gimg_ref, True,
            lambda v, rows, lanes: (v + cot2[0, rows, lanes].astype(F32)).astype(BF16),
        )

        @pl.when(i == 0)
        def _():
            reduce_third()

        @pl.when(i == 3)
        def _():
            wait_all(kx_copies())
            total = kall[pl.ds(pl.multiple_of(at.core * 32 + at.x * 8, 8), 8), :]
            for j in range(7):
                total = total + krx[j]
            ky[at.y] = total
            start_all(ky_copies())

        @pl.when(i == 9)
        def _():
            wait_all(ky_copies())
            kz[at.z] = ky[0] + ky[1] + ky[2] + ky[3]
            start_all(kz_copies())
            reduce_end()
            far_start()

        return carry

    lax.fori_loop(0, 12, backward, 0)
    gimg_copy = pltpu.make_async_copy(gimg_ref, gimg_hbm, lsem.at[3])
    gimg_copy.start()
    wait_all(kz_copies())
    total = kz[0]
    for i in range(1, 8):
        total = total + kz[i]
    finf[pl.ds(pl.multiple_of(at.core * 32 + at.x * 8, 8), 8), :] = total
    start_all(kg_copies())

    @pl.when(at.source)
    def _():
        far_copy().wait()
        for side, ref in ((0, ge_ref), (1, gc_ref)):
            for part in range(3):
                total = fin[0, side, part].astype(F32) + fin[1, side, part].astype(F32)
                ref[part * ROWS : (part + 1) * ROWS, :] = total * scale
        for cp in near_copies():
            cp.start()

    wait_all(kg_copies())
    for i in range(7):
        gker_ref[i] = finf[7 * i : 7 * i + 7, :] * scale

    @pl.when(at.source)
    def _():
        for cp in near_copies():
            cp.wait_send()

    @pl.when(at.other)
    def _():
        for cp in near_copies():
            cp.wait_recv()

    block_copy.wait()
    gimg_copy.wait()


def hand_over(*refs):
    n = len(refs) // 3
    sem = refs[-1]
    loads = [pltpu.make_async_copy(refs[i], refs[2 * n + i], sem.at[0, i]) for i in range(n)]
    stores = [pltpu.make_async_copy(refs[2 * n + i], refs[n + i], sem.at[1, i]) for i in range(n)]
    for cp in loads:
        cp.start()
    for load, store in zip(loads, stores):
        load.wait()
        store.start()
    for cp in stores:
        cp.wait()


def per_device(images, cotangent, dw_kernel, w_expand, w_contract):
    vmem = lambda: pl.BlockSpec(memory_space=pltpu.VMEM)
    anywhere = lambda: pl.BlockSpec(memory_space=pl.ANY)
    scratch = [
        pltpu.VMEM((TOK, C), BF16),
        pltpu.VMEM((TOK, C), BF16),
        pltpu.VMEM((TOK, C), BF16),
        pltpu.VMEM((2, 96, ROWS, C), BF16),
        pltpu.VMEM((2, 96, ROWS, C), BF16),
        pltpu.VMEM((2, TOK, C), BF16),
        pltpu.VMEM((2, TOK, C), BF16),
        pltpu.VMEM((2, TOK, C), F32),
        pltpu.VMEM((2, TOK, C), F32),
        pltpu.VMEM((2, TOK, C), BF16),
        pltpu.VMEM((2, TOK, C), BF16),
        pltpu.VMEM((TOK, C), F32),
        pltpu.VMEM((TOK, 128), F32),
        pltpu.VMEM((22, 32, 128), F32),
        pltpu.VMEM((49, 8, C), F32),
        pltpu.VMEM((64, C), F32),
                pltpu.VMEM((7, 8, C), F32),
        pltpu.VMEM((4, 8, C), F32),
        pltpu.VMEM((8, 8, C), F32),
        pltpu.VMEM((2, 2, 3, ROWS, C), BF16),
        pltpu.VMEM((64, C), F32),
    ]
    for part in range(3):
        for phase in range(3):
            scratch.append(pltpu.VMEM((3, 2, sizes(part)[phase], ROWS, C), BF16))
    for part in range(3):
        for phase in range(3):
            scratch.append(pltpu.VMEM((2, sizes(part)[phase], ROWS, C), BF16))
    scratch += [pltpu.SemaphoreType.DMA((3, 3, SPLIT, 4))] * 4
    scratch += [pltpu.SemaphoreType.DMA((4,))] * 2
    scratch += [pltpu.SemaphoreType.DMA((24,))] * 2
    scratch += [pltpu.SemaphoreType.DMA((3,))] * 2
    scratch += [pltpu.SemaphoreType.DMA((4,))]
    shapes = (
        jax.ShapeDtypeStruct((TOK, C), BF16),
        jax.ShapeDtypeStruct((TOK, C), BF16),
        jax.ShapeDtypeStruct((7, 7, C), F32),
        jax.ShapeDtypeStruct((48, C), F32),
        jax.ShapeDtypeStruct((48, C), F32),
    )
    results = pl.pallas_call(
        kernel,
        name="block_step",
        out_shape=shapes,
        in_specs=[anywhere(), anywhere(), vmem(), vmem(), vmem()],
        out_specs=(anywhere(), anywhere(), vmem(), vmem(), vmem()),
        scratch_shapes=scratch,
        compiler_params=pltpu.CompilerParams(
            collective_id=0, has_side_effects=True, vmem_limit_bytes=60 * 2**20
        ),
        cost_estimate=pl.CostEstimate(flops=15 * 10**9, bytes_accessed=10**7, transcendentals=10**6),
    )(
        images.reshape(TOK, C),
        cotangent.reshape(TOK, C),
        dw_kernel,
        w_expand,
        w_contract,
    )
    out, gimg, gker, ge, gc = pl.pallas_call(
        hand_over,
        name="hand_over",
        out_shape=shapes,
        in_specs=[anywhere() for _ in range(5)],
        out_specs=tuple(anywhere() for _ in range(5)),
        scratch_shapes=[pltpu.VMEM(a.shape, a.dtype) for a in shapes] + [pltpu.SemaphoreType.DMA((2, 5))],
    )(*results)
    return out.reshape(images.shape), gimg.reshape(images.shape), gker, ge, gc


def solution(mesh):
    tokens = P(("grp", "dev"), None, None, None)
    rows = P("dev", None)
    return jax.shard_map(
        per_device,
        mesh=mesh,
        in_specs=(tokens, tokens, P(), rows, rows),
        out_specs=(tokens, tokens, P(), rows, rows),
        check_vma=False,
    )
```

time: 121 us -> 99.2 us (0.82)
  Pallas kernels: 112 us -> 98.4 us
  local copies, waits for them, and re-layouts: 8.01 us -> 0 us
    pallas_call x1 -> x2, Pallas kernels: 112 us -> 98.4 us  [the longest x1 95.9 us: per_device(): pl.pallas_call(kernel, name='block_step', out_shape=shapes, in_specs=[any...]
    unnamed x10 -> x0, local copies, waits for them, and re-layouts: 4.8 us -> none
    reshape x2 -> x0, local copies, waits for them, and re-layouts: 3.22 us -> none  [the longest x1 1.61 us: per_device(): dw_kernel.reshape(49, C)]
where the time goes in v2:
time: 99.2 us; the launch traced here: 99.1 us
  Pallas kernels  98.4 us (99%)
    pallas_call x1, Pallas kernels, per_device(): pl.pallas_call(kernel, name='block_step', out_shape=shapes, in_specs=[any...  95.9 us
    pallas_call x1, Pallas kernels, per_device(): pl.pallas_call(hand_over, name='hand_over', out_shape=shapes, in_specs=[a...  2.51 us

profile of v2, /device:TPU:1, one launch (start us, length us, event | category | flops | bytes accessed | tf_op | source)
XLA Modules:
  0.0 99.1 jit_solution(15656240343642304565)
XLA Ops:
  0.6 95.9 %block_step.1 = (bf16[512,768]{1,0:T(8,128)(2,1)}, bf16[512,768]{1,0:T(8,128)(2,1)}, f32[7,7,768]{2,1,0:T(8,128)}, f32[48,768]{1,0:T(8,128)}, f32[48,768]{1,0:T(8,128)}) custom-call(bf16[512,768]{1,0:T(8,128)(2,1)} %bitcast.4, bf16[512,768]{1,0:T(8,128)(2,1)} %bitcast.5, f32[7,7,768]{2,1,0:T(8,128)} %dwk_ref.1, bf16[48,768]{1,0:T(8,128)(2,1)} %we_ref.1, ...), custom_call_target="tpu_custom_call" | custom-call | flops 15000000512 | bytes 10000000 | tf_op jit(solution)/shard_map/block_step/pallas_call | solution.py:661
  96.6 2.5 %hand_over.1 = (bf16[512,768]{1,0:T(8,128)(2,1)}, bf16[512,768]{1,0:T(8,128)(2,1)}, f32[7,7,768]{2,1,0:T(8,128)}, f32[48,768]{1,0:T(8,128)}, f32[48,768]{1,0:T(8,128)}) custom-call(bf16[512,768]{1,0:T(8,128)(2,1)} %get-tuple-element.15.refs_0_, bf16[512,768]{1,0:T(8,128)(2,1)} %get-tuple-element.16.refs_1_, f32[7,7,768]{2,1,0:T(8,128)} %get-tuple-element.17.refs_2_, ...), custom_call_target="tpu_custom_call" | custom-call | tf_op jit(solution)/shard_map/hand_over/pallas_call | solution.py:679

commit v3 on v2

--- a/solution.py
+++ b/solution.py
@@ -105,7 +105,7 @@
     img_hbm, cot_hbm, dwk_ref, we_ref, wc_ref,
     out_hbm, gimg_hbm, gker_ref, ge_ref, gc_ref,
     img_ref, out_ref, gimg_ref, buf, grads, nrm2, cot2, mix, ngr, ex_send, ex_recv, conv, inv, pad, kacc,
-    kall, krx, ky, kz, fin, finf,
+    kall, krx, ky, kz, fin, finf, acts,
     rb0, rb1, rb2, rb3, rb4, rb5, rb6, rb7, rb8,
     t0, t1, t2, t3, t4, t5, t6, t7, t8,
     bsem_s, bsem_r, rsem_s, rsem_r, esem_s, esem_r, ksem_s, ksem_r, fsem_s, fsem_r, lsem,
@@ -121,10 +121,11 @@
     friends += [at.peer("x", o, 1 - at.core) for o in (1, -1, 2)]
     for friend in friends:
         pl.semaphore_signal(barrier, inc=1, device_id=friend, device_id_type=MESH)
-    img_in = pltpu.make_async_copy(img_hbm, img_ref, lsem.at[0])
-    cot_in = pltpu.make_async_copy(cot_hbm, cot2.at[0], lsem.at[1])
-    img_in.start()
-    cot_in.start()
+    quarters = [pl.ds(i * 128, 128) for i in range(4)]
+    img_in = [pltpu.make_async_copy(img_hbm.at[q], img_ref.at[q], lsem.at[0, i]) for i, q in enumerate(quarters)]
+    cot_in = [pltpu.make_async_copy(cot_hbm.at[q], cot2.at[0, q], lsem.at[1, i]) for i, q in enumerate(quarters)]
+    for cp in img_in + cot_in:
+        cp.start()
     pl.semaphore_wait(barrier, len(friends))
 
     def copy(src, dst, send, recv, to):
@@ -133,17 +134,24 @@
             device_id=to, device_id_type=MESH,
         )
 
-    def gather_copies(part, phase, step=None):
+    def gather_copies(part, phase, step=None, kind=None):
         axis = ORDERS[part][phase]
         px = ORDERS[part].index("x")
         if phase == 2:
-            share = at.share(part, step)
-            runs = [(step, (where(part, share, at.slot(axis)), sizes(part)[2] // SPLIT))]
+            share, count = at.share(part, step), sizes(part)[2] // SPLIT
+            runs = [(step, (where(part, share, at.slot(axis)), count))]
         else:
             runs = enumerate(at.runs(part, phase))
+        if kind == "pass":
+            out = []
+            for off, half, j in ((1, 0, 2), (-1, 1, 3)):
+                ref = buf.at[half, pl.ds(where(part, share, at.slot(axis, -off)), count)]
+                cp = copy(ref, ref, bsem_s.at[part, phase, step, j], bsem_r.at[part, phase, step, j], at.peer(axis, off))
+                out.append((cp, at.other if axis == "x" else None, at.source if axis == "x" else None))
+            return out
         out = []
         for r, (start, count) in runs:
-            for off, half, j in moves(axis):
+            for off, half, j in moves(axis)[: 2 if kind == "near" else 4]:
                 if half is None:
                     ref = buf.at[:, pl.ds(start, count)]
                 else:
@@ -159,12 +167,12 @@
                 out.append((cp, send_if, recv_if))
         return out
 
-    def gather_start(part, phase, step=None):
-        for cp, send_if, _ in gather_copies(part, phase, step):
+    def gather_start(part, phase, step=None, kind=None):
+        for cp, send_if, _ in gather_copies(part, phase, step, kind):
             when(send_if, cp.start)
 
-    def gather_wait(part, phase, step=None):
-        for cp, send_if, recv_if in gather_copies(part, phase, step):
+    def gather_wait(part, phase, step=None, kind=None):
+        for cp, send_if, recv_if in gather_copies(part, phase, step, kind):
             when(send_if, cp.wait_send)
             when(recv_if, cp.wait_recv)
 
@@ -179,7 +187,7 @@
         @pl.when(at.source)
         def _():
             gather_start(2, 2, 0)
-            gather_start(2, 2, 1)
+            gather_start(2, 2, 1, "near")
 
     def gather_third():
         for part in range(3):
@@ -189,16 +197,21 @@
         def _():
             gather_start(2, 2, 0)
 
-        gather_start(0, 2, 1)
-        gather_start(1, 2, 1)
+        gather_start(0, 2, 1, "near")
+        gather_start(1, 2, 1, "near")
 
         @pl.when(at.other)
         def _():
-            gather_start(2, 2, 1)
+            gather_start(2, 2, 1, "near")
 
         for step in range(2, SPLIT):
             for part in range(3):
-                gather_start(part, 2, step)
+                gather_start(part, 2, step, "near")
+
+    def gather_pass(step):
+        for part in range(3):
+            gather_wait(part, 2, step, "near")
+            gather_start(part, 2, step, "pass")
 
     @pl.when(at.source)
     def _():
@@ -213,7 +226,8 @@
     cot_copy.start()
 
     pad[...] = jnp.zeros_like(pad)
-    img_in.wait()
+    for cp in img_in:
+        cp.wait()
 
     def windows(values):
         pad[3:19, 8:24, :] = values.reshape(16, 16, 128)
@@ -260,7 +274,8 @@
     nrm_copy = copy(nrm2.at[0], nrm2.at[1], esem_s.at[1], esem_r.at[1], partner)
     nrm_copy.start()
     gather_third()
-    cot_in.wait()
+    for cp in cot_in:
+        cp.wait()
     cot_copy.wait()
     nrm_copy.wait()
 
@@ -383,9 +398,25 @@
     count = 32 // SPLIT
     width = 3 * count * ROWS
 
+    def mix_step(step, carry):
+        here = [pl.ds(where(part, at.share(part, step), 0), count) for part in range(3)]
+        contract = jnp.concatenate([buf[1, h] for h in here]).reshape(width, C)
+        mix[...] += dot(acts[step], contract, NN).reshape(2, TOK, C)
+        return carry
+
+    for part in range(3):
+        gather_wait(part, 2, 0)
+
     def share_step(step, carry):
-        for part in range(3):
-            gather_wait(part, 2, step)
+        @pl.when(step == 1)
+        def _():
+            gather_pass(2)
+
+        @pl.when(step >= 1)
+        def _():
+            for part in range(3):
+                gather_wait(part, 2, step, "pass")
+
         normed = nrm2[...].reshape(2 * TOK, C)
         upstream = cot2[...].reshape(2 * TOK, C)
         here = [pl.ds(where(part, at.share(part, step), 0), count) for part in range(3)]
@@ -402,9 +433,14 @@
         for part in range(3):
             grads[0, here[part]] = grad_e[part]
             grads[1, here[part]] = grad_c[part]
+        acts[step] = activated
+
+        @pl.when(step <= 1)
+        def _():
+            gather_pass(2 * step + 1)
+
         reduce_start_last(step)
         ngr[...] += dot(pre_grad, expand, NN).reshape(2, TOK, C)
-        mix[...] += dot(activated, contract, NN).reshape(2, TOK, C)
 
         @pl.when(step >= 2)
         def _():
@@ -425,7 +461,8 @@
         return cp
 
     ngr_copy = send_back(0, ngr)
-    mix_copy = send_back(1, mix)
+
+    lax.fori_loop(0, 2, mix_step, 0)
     ngr_copy.wait()
     def norm_back(i, carry):
         rows = pl.ds(pl.multiple_of(i * 64, 64), 64)
@@ -439,9 +476,9 @@
     lax.fori_loop(0, 8, norm_back, 0)
 
     def kernel_terms(block, carry):
-        @pl.when(block % 3 == 0)
-        def _():
-            reduce_second(2 + block // 3)
+        @pl.when(jnp.logical_or(block == 0, block == 4))
+        def _():
+            reduce_second(2 + block // 4)
 
         lanes = pl.ds(pl.multiple_of(block * 128, 128), 128)
         for image in range(2):
@@ -501,16 +538,6 @@
             cp.wait()
 
     start_all(kx_copies())
-    mix_copy.wait()
-
-    def block_out(i, carry):
-        rows = pl.ds(pl.multiple_of(i * 64, 64), 64)
-        out_ref[rows, :] = (mix[0, rows, :] + ex_recv[1, rows, :].astype(F32)).astype(BF16)
-        return carry
-
-    lax.fori_loop(0, 8, block_out, 0)
-    block_copy = pltpu.make_async_copy(out_ref, out_hbm, lsem.at[2])
-    block_copy.start()
 
     scale = float(TOK * 256) ** (-0.5)
 
@@ -519,11 +546,8 @@
     def far_copy():
         return copy(fin.at[at.hi], fin.at[at.hi], fsem_s.at[0], fsem_r.at[0], far)
 
-    def near_copies():
-        return [
-            copy(ge_ref, ge_ref, fsem_s.at[1], fsem_r.at[1], partner),
-            copy(gc_ref, gc_ref, fsem_s.at[2], fsem_r.at[2], partner),
-        ]
+    def near_copy(half):
+        return copy(fin.at[half], fin.at[half], fsem_s.at[half + 1], fsem_r.at[half + 1], partner)
 
     def far_start():
         @pl.when(at.source)
@@ -532,6 +556,7 @@
                 for side in range(2):
                     fin[at.hi, side, part] = tbufs[part][0][side, 0]
             far_copy().start()
+            near_copy(at.hi).start()
 
     def backward(i, carry):
         conv_step(
@@ -539,11 +564,11 @@
             lambda v, rows, lanes: (v + cot2[0, rows, lanes].astype(F32)).astype(BF16),
         )
 
-        @pl.when(i == 0)
+        @pl.when(i == 5)
         def _():
             reduce_third()
 
-        @pl.when(i == 3)
+        @pl.when(i == 6)
         def _():
             wait_all(kx_copies())
             total = kall[pl.ds(pl.multiple_of(at.core * 32 + at.x * 8, 8), 8), :]
@@ -552,50 +577,53 @@
             ky[at.y] = total
             start_all(ky_copies())
 
-        @pl.when(i == 9)
-        def _():
-            wait_all(ky_copies())
-            kz[at.z] = ky[0] + ky[1] + ky[2] + ky[3]
-            start_all(kz_copies())
-            reduce_end()
-            far_start()
-
         return carry
 
     lax.fori_loop(0, 12, backward, 0)
-    gimg_copy = pltpu.make_async_copy(gimg_ref, gimg_hbm, lsem.at[3])
+    gimg_copy = pltpu.make_async_copy(gimg_ref, gimg_hbm, lsem.at[3, 0])
     gimg_copy.start()
+    mix_step(2, 0)
+    wait_all(ky_copies())
+    kz[at.z] = ky[0] + ky[1] + ky[2] + ky[3]
+    start_all(kz_copies())
+    reduce_end()
+    far_start()
+    mix_step(3, 0)
+    mix_copy = send_back(1, mix)
     wait_all(kz_copies())
     total = kz[0]
     for i in range(1, 8):
         total = total + kz[i]
     finf[pl.ds(pl.multiple_of(at.core * 32 + at.x * 8, 8), 8), :] = total
     start_all(kg_copies())
+    mix_copy.wait()
+
+    def block_out(i, carry):
+        rows = pl.ds(pl.multiple_of(i * 64, 64), 64)
+        out_ref[rows, :] = (mix[0, rows, :] + ex_recv[1, rows, :].astype(F32)).astype(BF16)
+        return carry
+
+    lax.fori_loop(0, 8, block_out, 0)
+    block_copy = pltpu.make_async_copy(out_ref, out_hbm, lsem.at[2, 0])
+    block_copy.start()
+
 
     @pl.when(at.source)
     def _():
         far_copy().wait()
-        for side, ref in ((0, ge_ref), (1, gc_ref)):
-            for part in range(3):
-                total = fin[0, side, part].astype(F32) + fin[1, side, part].astype(F32)
-                ref[part * ROWS : (part + 1) * ROWS, :] = total * scale
-        for cp in near_copies():
-            cp.start()
+        near_copy(1 - at.hi).start()
 
     wait_all(kg_copies())
     for i in range(7):
         gker_ref[i] = finf[7 * i : 7 * i + 7, :] * scale
 
-    @pl.when(at.source)
-    def _():
-        for cp in near_copies():
-            cp.wait_send()
-
-    @pl.when(at.other)
-    def _():
-        for cp in near_copies():
-            cp.wait_recv()
-
+    for half in range(2):
+        when(at.source, near_copy(half).wait_send)
+        when(at.other, near_copy(half).wait_recv)
+    for side, ref in ((0, ge_ref), (1, gc_ref)):
+        for part in range(3):
+            total = fin[0, side, part].astype(F32) + fin[1, side, part].astype(F32)
+            ref[part * ROWS : (part + 1) * ROWS, :] = total * scale
     block_copy.wait()
     gimg_copy.wait()
 
@@ -603,8 +631,15 @@
 def hand_over(*refs):
     n = len(refs) // 3
     sem = refs[-1]
-    loads = [pltpu.make_async_copy(refs[i], refs[2 * n + i], sem.at[0, i]) for i in range(n)]
-    stores = [pltpu.make_async_copy(refs[2 * n + i], refs[n + i], sem.at[1, i]) for i in range(n)]
+    loads, stores = [], []
+    for i in range(n):
+        rows = refs[i].shape[0]
+        step = 128 if rows == TOK else rows
+        for k in range(0, rows, step):
+            part = pl.ds(k, step)
+            a, b, c = refs[i].at[part], refs[2 * n + i].at[part], refs[n + i].at[part]
+            loads.append(pltpu.make_async_copy(a, b, sem.at[0, len(loads)]))
+            stores.append(pltpu.make_async_copy(b, c, sem.at[1, len(stores)]))
     for cp in loads:
         cp.start()
     for load, store in zip(loads, stores):
@@ -639,6 +674,7 @@
         pltpu.VMEM((8, 8, C), F32),
         pltpu.VMEM((2, 2, 3, ROWS, C), BF16),
         pltpu.VMEM((64, C), F32),
+        pltpu.VMEM((SPLIT, 2 * TOK, 3 * (32 // SPLIT) * ROWS), BF16),
     ]
     for part in range(3):
         for phase in range(3):
@@ -650,7 +686,7 @@
     scratch += [pltpu.SemaphoreType.DMA((4,))] * 2
     scratch += [pltpu.SemaphoreType.DMA((24,))] * 2
     scratch += [pltpu.SemaphoreType.DMA((3,))] * 2
-    scratch += [pltpu.SemaphoreType.DMA((4,))]
+    scratch += [pltpu.SemaphoreType.DMA((4, 4))]
     shapes = (
         jax.ShapeDtypeStruct((TOK, C), BF16),
         jax.ShapeDtypeStruct((TOK, C), BF16),
@@ -682,7 +718,7 @@
         out_shape=shapes,
         in_specs=[anywhere() for _ in range(5)],
         out_specs=tuple(anywhere() for _ in range(5)),
-        scratch_shapes=[pltpu.VMEM(a.shape, a.dtype) for a in shapes] + [pltpu.SemaphoreType.DMA((2, 5))],
+        scratch_shapes=[pltpu.VMEM(a.shape, a.dtype) for a in shapes] + [pltpu.SemaphoreType.DMA((2, 11))],
     )(*results)
     return out.reshape(images.shape), gimg.reshape(images.shape), gker, ge, gc
 

time: 99.2 us -> 91.5 us (0.922)
  Pallas kernels: 98.4 us -> 90.6 us
    pallas_call x1, Pallas kernels: 95.9 us -> 88.1 us  [per_device(): pl.pallas_call(kernel, name='block_step', out_shape=shapes, in_specs=[any...]
where the time goes in v3:
time: 91.5 us; the launch traced here: 91.4 us
  Pallas kernels  90.6 us (99%)
    pallas_call x1, Pallas kernels, per_device(): pl.pallas_call(kernel, name='block_step', out_shape=shapes, in_specs=[any...  88.1 us
    pallas_call x1, Pallas kernels, per_device(): pl.pallas_call(hand_over, name='hand_over', out_shape=shapes, in_specs=[a...  2.5 us

profile of v3, /device:TPU:1, one launch (start us, length us, event | category | flops | bytes accessed | tf_op | source)
XLA Modules:
  0.0 91.4 jit_solution(17322276303374949465)
XLA Ops:
  0.6 88.1 %block_step.1 = (bf16[512,768]{1,0:T(8,128)(2,1)}, bf16[512,768]{1,0:T(8,128)(2,1)}, f32[7,7,768]{2,1,0:T(8,128)}, f32[48,768]{1,0:T(8,128)}, f32[48,768]{1,0:T(8,128)}) custom-call(bf16[512,768]{1,0:T(8,128)(2,1)} %bitcast.4, bf16[512,768]{1,0:T(8,128)(2,1)} %bitcast.5, f32[7,7,768]{2,1,0:T(8,128)} %dwk_ref.1, bf16[48,768]{1,0:T(8,128)(2,1)} %we_ref.1, ...), custom_call_target="tpu_custom_call" | custom-call | flops 15000000512 | bytes 10000000 | tf_op jit(solution)/shard_map/block_step/pallas_call | solution.py:697
  88.7 2.5 %hand_over.1 = (bf16[512,768]{1,0:T(8,128)(2,1)}, bf16[512,768]{1,0:T(8,128)(2,1)}, f32[7,7,768]{2,1,0:T(8,128)}, f32[48,768]{1,0:T(8,128)}, f32[48,768]{1,0:T(8,128)}) custom-call(bf16[512,768]{1,0:T(8,128)(2,1)} %get-tuple-element.15.refs_0_, bf16[512,768]{1,0:T(8,128)(2,1)} %get-tuple-element.16.refs_1_, f32[7,7,768]{2,1,0:T(8,128)} %get-tuple-element.17.refs_2_, ...), custom_call_target="tpu_custom_call" | custom-call | tf_op jit(solution)/shard_map/hand_over/pallas_call | solution.py:715

commit v4 on v3

--- a/solution.py
+++ b/solution.py
@@ -102,9 +102,9 @@
 
 
 def kernel(
-    img_hbm, cot_hbm, dwk_ref, we_ref, wc_ref,
+    img_hbm, cot_hbm, dwk_hbm, we_hbm, wc_hbm,
     out_hbm, gimg_hbm, gker_ref, ge_ref, gc_ref,
-    img_ref, out_ref, gimg_ref, buf, grads, nrm2, cot2, mix, ngr, ex_send, ex_recv, conv, inv, pad, kacc,
+    img_ref, out_ref, gimg_ref, dwk_ref, we_ref, wc_ref, buf, grads, nrm2, cot2, mix, ngr, ex_send, ex_recv, conv, inv, pad, kacc,
     kall, krx, ky, kz, fin, finf, acts,
     rb0, rb1, rb2, rb3, rb4, rb5, rb6, rb7, rb8,
     t0, t1, t2, t3, t4, t5, t6, t7, t8,
@@ -124,7 +124,9 @@
     quarters = [pl.ds(i * 128, 128) for i in range(4)]
     img_in = [pltpu.make_async_copy(img_hbm.at[q], img_ref.at[q], lsem.at[0, i]) for i, q in enumerate(quarters)]
     cot_in = [pltpu.make_async_copy(cot_hbm.at[q], cot2.at[0, q], lsem.at[1, i]) for i, q in enumerate(quarters)]
-    for cp in img_in + cot_in:
+    w_in = [pltpu.make_async_copy(we_hbm, we_ref, lsem.at[4, 0]), pltpu.make_async_copy(wc_hbm, wc_ref, lsem.at[4, 1])]
+    dwk_in = pltpu.make_async_copy(dwk_hbm, dwk_ref, lsem.at[4, 2])
+    for cp in w_in + img_in + [dwk_in] + cot_in:
         cp.start()
     pl.semaphore_wait(barrier, len(friends))
 
@@ -213,6 +215,9 @@
             gather_wait(part, 2, step, "near")
             gather_start(part, 2, step, "pass")
 
+    for cp in w_in:
+        cp.wait()
+
     @pl.when(at.source)
     def _():
         for part in range(3):
@@ -226,7 +231,7 @@
     cot_copy.start()
 
     pad[...] = jnp.zeros_like(pad)
-    for cp in img_in:
+    for cp in img_in + [dwk_in]:
         cp.wait()
 
     def windows(values):
@@ -518,7 +523,7 @@
     def kz_copies():
         return [
             copy(kz.at[at.z], kz.at[at.z], ksem_s.at[10 + j], ksem_r.at[10 + j], at.peer("z", off))
-            for j, off in enumerate(range(1, 8))
+            for j, off in enumerate((4, 3, 5, 2, 6, 1, 7))
         ]
 
     share = pl.ds(at.core * 32 + at.x * 8, 8)
@@ -582,12 +587,12 @@
     lax.fori_loop(0, 12, backward, 0)
     gimg_copy = pltpu.make_async_copy(gimg_ref, gimg_hbm, lsem.at[3, 0])
     gimg_copy.start()
-    mix_step(2, 0)
     wait_all(ky_copies())
     kz[at.z] = ky[0] + ky[1] + ky[2] + ky[3]
     start_all(kz_copies())
     reduce_end()
     far_start()
+    mix_step(2, 0)
     mix_step(3, 0)
     mix_copy = send_back(1, mix)
     wait_all(kz_copies())
@@ -656,6 +661,9 @@
         pltpu.VMEM((TOK, C), BF16),
         pltpu.VMEM((TOK, C), BF16),
         pltpu.VMEM((TOK, C), BF16),
+        pltpu.VMEM((7, 7, C), F32),
+        pltpu.VMEM((48, C), BF16),
+        pltpu.VMEM((48, C), BF16),
         pltpu.VMEM((2, 96, ROWS, C), BF16),
         pltpu.VMEM((2, 96, ROWS, C), BF16),
         pltpu.VMEM((2, TOK, C), BF16),
@@ -686,7 +694,7 @@
     scratch += [pltpu.SemaphoreType.DMA((4,))] * 2
     scratch += [pltpu.SemaphoreType.DMA((24,))] * 2
     scratch += [pltpu.SemaphoreType.DMA((3,))] * 2
-    scratch += [pltpu.SemaphoreType.DMA((4, 4))]
+    scratch += [pltpu.SemaphoreType.DMA((5, 4))]
     shapes = (
         jax.ShapeDtypeStruct((TOK, C), BF16),
         jax.ShapeDtypeStruct((TOK, C), BF16),
@@ -698,7 +706,7 @@
         kernel,
         name="block_step",
         out_shape=shapes,
-        in_specs=[anywhere(), anywhere(), vmem(), vmem(), vmem()],
+        in_specs=[anywhere() for _ in range(5)],
         out_specs=(anywhere(), anywhere(), vmem(), vmem(), vmem()),
         scratch_shapes=scratch,
         compiler_params=pltpu.CompilerParams(

time: 91.5 us -> 90.7 us (level)
  no operation moved by 1% of the time
where the time goes in v4:
time: 90.7 us; the launch traced here: 90.6 us
  Pallas kernels  89.8 us (99%)
    pallas_call x1, Pallas kernels, per_device(): pl.pallas_call(kernel, name='block_step', out_shape=shapes, in_specs=[any...  87.3 us
    pallas_call x1, Pallas kernels, per_device(): pl.pallas_call(hand_over, name='hand_over', out_shape=shapes, in_specs=[a...  2.5 us

profile of v4, /device:TPU:1, one launch (start us, length us, event | category | flops | bytes accessed | tf_op | source)
XLA Modules:
  0.0 90.6 jit_solution(15633420466340848660)
XLA Ops:
  0.6 87.3 %block_step.1 = (bf16[512,768]{1,0:T(8,128)(2,1)}, bf16[512,768]{1,0:T(8,128)(2,1)}, f32[7,7,768]{2,1,0:T(8,128)}, f32[48,768]{1,0:T(8,128)}, f32[48,768]{1,0:T(8,128)}) custom-call(bf16[512,768]{1,0:T(8,128)(2,1)} %bitcast.4, bf16[512,768]{1,0:T(8,128)(2,1)} %bitcast.5, f32[7,7,768]{2,1,0:T(8,128)} %dwk_hbm.1, bf16[48,768]{1,0:T(8,128)(2,1)} %we_hbm.1, ...), custom_call_target="tpu_custom_call" | custom-call | flops 15000000512 | bytes 10000000 | tf_op jit(solution)/shard_map/block_step/pallas_call | solution.py:705
  87.9 2.5 %hand_over.1 = (bf16[512,768]{1,0:T(8,128)(2,1)}, bf16[512,768]{1,0:T(8,128)(2,1)}, f32[7,7,768]{2,1,0:T(8,128)}, f32[48,768]{1,0:T(8,128)}, f32[48,768]{1,0:T(8,128)}) custom-call(bf16[512,768]{1,0:T(8,128)(2,1)} %get-tuple-element.15.refs_0_, bf16[512,768]{1,0:T(8,128)(2,1)} %get-tuple-element.16.refs_1_, f32[7,7,768]{2,1,0:T(8,128)} %get-tuple-element.17.refs_2_, ...), custom_call_target="tpu_custom_call" | custom-call | tf_op jit(solution)/shard_map/hand_over/pallas_call | solution.py:723
